TPU v7x, 128 devices: a whole 4x4x4 slice. The times are simulated.
128 devices in a mesh: lon: 32 (over z_hi, x, y), lat: 4 (over z_lo, core).
Axes of the slice: x: 4, y: 4, z: 4 (z_hi: 2, z_lo: 2; z = z_hi * 2 + z_lo), core: 2. Of those that a mesh axis runs over, the one named last changes fastest.
Arguments:
- patch_rows: bfloat16 [262144, 512], P(('lon', 'lat')), may hold values from -400 to 400
- source_embed: bfloat16 [4, 512], replicated, may hold values from -6 to 6
- cell_embed: bfloat16 [512, 128, 512], P('lon', 'lat'), may hold values from -6 to 6
- level_query: bfloat16 [4, 512], replicated, may hold values from -6 to 6
- margin_rows: int32 [128, 3, 3, 128], P(('lon', 'lat')), may hold values from 0 to 2047, as said below
- margin_counts: int32 [128, 3, 3], P(('lon', 'lat')), may hold values from 0 to 128, as said below
- query_weight: bfloat16 [512, 512], replicated, may hold values from -0.25 to 0.25
- key_weight: bfloat16 [512, 512], replicated, may hold values from -0.25 to 0.25
- value_weight: bfloat16 [512, 512], replicated, may hold values from -0.25 to 0.25
- out_weight: bfloat16 [512, 512], replicated, may hold values from -0.25 to 0.25
- conv_weight: bfloat16 [2, 3, 3, 512, 512], replicated, may hold values from -0.09375 to 0.09375
Outputs:
- latent: bfloat16 [512, 128, 4, 512], P('lon', 'lat')
Inputs may be any that keep to these rules, and one draw needn't show every extreme that they name: margin_rows[s, a, b, j] is a local row of device s. `margin_counts`: a list whose source device lies outside the latitude range has count 0; every other list, the owner's own among them, has at least one live row; in every draw some tile owner receives 128 rows from every source device beside it.
All inputs are finite; a program needn't handle non-finite values.
Results may differ from a plain program's by a relative error of at most 0.009.
The roundings to bfloat16 on the way count: a program that leaves them out, or rounds other values in their place, can miss the bound.
Values may be sent and summed in bfloat16 or wider, within the bound.
No kernel may reach another device: no remote copies, remote signals or barrier semaphores. Data moves between devices by JAX's collectives and lax.ppermute only.
A program may use at most 192 MiB of HBM per device.

v0:
```python
import math

import jax
import jax.numpy as jnp
from jax import lax
from jax.sharding import PartitionSpec as P

HEADS = 16
SOURCES = 4
LEVELS = 4
LAYERS = 2


def with_halo(block, sides, width, periodic):
    for axis, dim in sides:
        count = lax.axis_size(axis)
        forward = [(i, i + 1) for i in range(count - 1)]
        if periodic:
            forward.append((count - 1, 0))
        backward = [(target, source) for source, target in forward]
        low = lax.ppermute(
            lax.slice_in_dim(block, block.shape[dim] - width, None, axis=dim), axis, forward
        )
        high = lax.ppermute(lax.slice_in_dim(block, 0, width, axis=dim), axis, backward)
        block = jnp.concatenate([low, block, high], axis=dim)
    return block


def shifted(value, axis, steps):
    count = lax.axis_size(axis)
    pairs = [(source, (source + steps) % count) for source in range(count)]
    return lax.ppermute(value, axis, pairs)


def shifted_2(block, axis, distance):
    devices = range(lax.axis_size(axis))
    route = [(i - distance, i) for i in devices if i - distance in devices]
    return lax.ppermute(block, axis, route)


def attend(latent_in, keys, values, valid, query_weight, out_weight):
    count = latent_in.shape[0]
    width = latent_in.shape[1]
    head_size = width // HEADS
    scale = 1.0 / math.sqrt(head_size)
    queries = jnp.dot(latent_in, query_weight, preferred_element_type=jnp.float32).astype(
        jnp.bfloat16
    )
    q_heads = queries.reshape(count, HEADS, head_size).transpose(1, 0, 2)
    k_heads = keys.reshape(-1, HEADS, head_size).transpose(1, 0, 2)
    v_heads = values.reshape(-1, HEADS, head_size).transpose(1, 0, 2)

    def one_head(operands):
        q_part, k_part, v_part = operands
        scores = (
            lax.dot_general(
                q_part, k_part, (((1,), (1,)), ((), ())), preferred_element_type=jnp.float32
            )
            * scale
        )
        scores = jnp.where(valid[None, :], scores, jnp.float32(-1e30))
        top = jnp.max(scores, axis=1, keepdims=True)
        weights = jnp.exp(scores - top)
        probs = (weights / jnp.sum(weights, axis=1, keepdims=True)).astype(jnp.bfloat16)
        return jnp.dot(probs, v_part, preferred_element_type=jnp.float32).astype(jnp.bfloat16)

    heads_out = lax.map(one_head, (q_heads, k_heads, v_heads))
    attended = heads_out.transpose(1, 0, 2).reshape(count, width)
    mixed = latent_in.astype(jnp.float32) + jnp.dot(
        attended, out_weight, preferred_element_type=jnp.float32
    )
    return mixed.astype(jnp.bfloat16)


def conv_taps(padded, kernels, cells_lon, cells_lat):
    width = padded.shape[-1]
    total = jnp.zeros((cells_lon * cells_lat * padded.shape[2], width), jnp.float32)
    for row_off in range(3):
        for col_off in range(3):
            window = padded[row_off : row_off + cells_lon, col_off : col_off + cells_lat].reshape(
                -1, width
            )
            total = total + jnp.dot(
                window, kernels[row_off, col_off], preferred_element_type=jnp.float32
            )
    return total.reshape(cells_lon, cells_lat, padded.shape[2], width)


def conv_layer(state, kernels, cos_gain, lat_place, lat_count, lon_count):
    values = state.astype(jnp.float32)
    spread = jnp.sqrt(jnp.mean(values * values, axis=-1, keepdims=True) + 1e-06)
    scaled = (values / spread * cos_gain[None, :, None, None]).astype(jnp.bfloat16)
    lon_ext = with_halo(scaled, (("lon", 0),), 1, True)
    full = with_halo(lon_ext, (("lat", 1),), 1, False)
    edges = jnp.stack([lon_ext[:, 0], lon_ext[:, -1]], axis=0)
    across = shifted(edges, "lon", lon_count // 2)
    top = jnp.where(lat_place == 0, across[0], full[:, 0])
    bottom = jnp.where(lat_place == lat_count - 1, across[1], full[:, -1])
    padded = jnp.concatenate([top[:, None], full[:, 1:-1], bottom[:, None]], axis=1)
    conv = conv_taps(padded, kernels, state.shape[0], state.shape[1])
    return (values + jax.nn.gelu(conv, approximate=False)).astype(jnp.bfloat16)


def shards(
    patch_rows,
    source_embed,
    cell_embed,
    level_query,
    margin_rows,
    margin_counts,
    query_weight,
    key_weight,
    value_weight,
    out_weight,
    conv_weight,
):
    lon_count = lax.axis_size("lon")
    lat_count = lax.axis_size("lat")
    capacity = margin_rows.shape[3]
    width = patch_rows.shape[1]
    rows = (
        patch_rows.reshape(SOURCES, -1, width).astype(jnp.float32)
        + source_embed.astype(jnp.float32)[:, None, :]
    )
    rows = rows.astype(jnp.bfloat16).reshape(-1, width)
    payload = jnp.take(rows, margin_rows.reshape(-1), axis=0).reshape(3, 3, capacity, rows.shape[1])
    early = [None, payload[1], None]
    for offset in (1, -1):
        early[1 - offset] = shifted(payload[1 + offset], "lon", offset)
    middle = jnp.stack(early, axis=0)
    late = [None, middle[:, 1], None]
    for offset in (1, -1):
        late[1 - offset] = shifted_2(middle[:, 1 + offset], "lat", offset)
    arrived = jnp.stack(late, axis=1)
    arrived = arrived.reshape(9 * capacity, rows.shape[1])
    counts_in = margin_counts.reshape(3, 3)
    valid = (jnp.arange(capacity, dtype=jnp.int32)[None, None, :] < counts_in[:, :, None]).reshape(
        -1
    )
    keys = jnp.dot(arrived, key_weight, preferred_element_type=jnp.float32).astype(jnp.bfloat16)
    vals = jnp.dot(arrived, value_weight, preferred_element_type=jnp.float32).astype(jnp.bfloat16)
    cells_lon = cell_embed.shape[0]
    cells_lat = cell_embed.shape[1]
    latent_in = (
        cell_embed[:, :, None, :].astype(jnp.float32) + level_query.astype(jnp.float32)[None, None]
    ).astype(jnp.bfloat16)
    latent_in = latent_in.reshape(-1, width)
    state = attend(latent_in, keys, vals, valid, query_weight, out_weight).reshape(
        cells_lon, cells_lat, LEVELS, width
    )
    lat_place = lax.axis_index("lat")
    rows_global = (lat_place * cells_lat + jnp.arange(cells_lat, dtype=jnp.int32)).astype(
        jnp.float32
    )
    phi = (rows_global + 0.5) / (cells_lat * lat_count) * jnp.pi - jnp.pi / 2
    cos_gain = 0.5 + jnp.cos(phi)
    for layer in range(LAYERS):
        state = conv_layer(state, conv_weight[layer], cos_gain, lat_place, lat_count, lon_count)
    return state


def solution(mesh):
    placed = (
        P(("lon", "lat"), None),
        P(),
        P("lon", "lat", None),
        P(),
        P(("lon", "lat"), None, None, None),
        P(("lon", "lat"), None, None),
        P(),
        P(),
        P(),
        P(),
        P(),
    )
    return jax.shard_map(
        shards, mesh=mesh, in_specs=placed, out_specs=P("lon", "lat", None, None), check_vma=False
    )
```

profile of v0, /device:TPU:1, one launch (start us, length us, event | category | flops | bytes accessed | tf_op | source)
XLA Modules:
  0.0 504.6 jit_solution(11433212321917599526)
XLA Ops:
  4.2 4.7 gather_fusion
  11.4 9.1 %collective-permute-start.1 = (bf16[3,128,512]{2,1,0:T(8,128)(2,1)}, bf16[3,128,512]{2,1,0:T(8,128)(2,1)}, u32[]{:S(2)}, u32[]{:S(2)}) collective-permute-start(bf16[3,128,512]{2,1,0:T(8,128)(2,1)} %bitcast.8), channel_id=1, source_target_pairs={{0,124},{4,0},{8,4},{12,8},{16,12},{20,16},{24,20},{28,24},{32,28}... | collective-permute-start | bytes 1179656 | tf_op jit(solution)/shard_map/ppermute | solution.py:32
  29.2 5.8 %copy.282 = bf16[2048,16,32]{2,0,1:T(8,128)(2,1)} copy(bf16[2048,16,32]{0,2,1:T(8,128)(2,1)S(1)} %bitcast.169) | data formatting | bytes 4194304 | tf_op jit(solution)/shard_map/reshape | solution.py:49
  37.5 4.4 collective-permute-start.2
  44.2 8.2 %slice_bitcast_fusion = (bf16[3,3,512,512]{3,2,1,0:T(8,128)(2,1)}, bf16[3,3,512,512]{3,2,1,0:T(8,128)(2,1)}) fusion(bf16[2,3,3,512,512]{4,3,2,1,0:T(8,128)(2,1)} %param.23), kind=kLoop, calls=%fused_computation.27 | loop fusion | bytes 18874368 | tf_op jit(solution)/shard_map/squeeze | solution.py:158
  54.4 3.4 copy.287
  57.8 3.3 copy.286
  61.1 124.0 %while.11 = (s32[]{:T(128)}, bf16[16,2048,32]{1,2,0:T(8,128)(2,1)}, bf16[16,2048,32]{2,1,0:T(8,128)(2,1)}, bf16[16,1152,32]{2,1,0:T(8,128)(2,1)}, bf16[16,1152,3...) while((s32[]{:T(128)}, bf16[16,2048,32]{1,2,0:T(8,128)(2,1)}, ...), condition=%wide.region_3.4_spmd.clone, body=%wide.region_0.3_spmd.clone.sunk | while | flops 320926848 | bytes 29604472 | solution.py:67
  65.6 3.3 fusion.114
  73.3 3.3 fusion.114
  81.1 3.3 fusion.114
  88.8 3.3 fusion.114
  96.5 3.3 fusion.114
  104.3 3.3 fusion.114
  112.0 3.3 fusion.114
  119.8 3.3 fusion.114
  127.5 3.3 fusion.114
  135.3 3.3 fusion.114
  143.0 3.3 fusion.114
  150.8 3.3 fusion.114
  158.5 3.3 fusion.114
  166.3 3.3 fusion.114
  174.0 3.3 fusion.114
  181.8 3.3 fusion.114
  185.1 3.7 multiply_reduce_fusion
  193.1 3.6 multiply_convert_fusion.1
  196.9 7.4 %collective-permute-start.5 = (bf16[1,32,4,512]{3,1,2,0:T(8,128)(2,1)S(1)}, bf16[1,32,4,512]{3,1,2,0:T(8,128)(2,1)S(1)}, u32[]{:S(2)}, u32[]{:S(2)}) collective-permute-start(bf16[1,32,4,512]{3,1,2,0:T(8,128)(2,1)S(1)} %get-tuple-element.104), channel_id=1, source_target_pairs={{4,0},{8,4},{12,8},{16,12},{20,16},{24,20},{28,24},{32,28},{36,32}... | collective-permute-start | bytes 393224 | tf_op jit(solution)/shard_map/ppermute | solution.py:24
  204.3 4.0 fusion.51
  208.5 4.2 collective-permute-start.7
  220.5 4.0 reshape.203
  224.5 5.1 %fusion.70 = f32[2048,512]{1,0:T(8,128)} fusion(bf16[2048,512]{1,0:T(8,128)(2,1)} %reshape.203, bf16[3,3,512,512]{3,2,1,0:T(8,128)(2,1)} %get-tuple-element.72), kind=kOutput, calls=%fused_computation.146 | convolution fusion | flops 1073741824 | bytes 6815744 | tf_op jit(solution)/shard_map/dot_general | solution.py:83
  232.6 4.0 reshape.208
  246.9 3.4 copy.297
  252.3 4.9 copy.295
  257.2 4.4 reshape.205
  261.6 3.4 fusion.79
  268.9 3.4 copy.299
  274.3 4.7 copy.296
  279.0 4.2 reshape.206
  283.2 5.1 %fusion.65 = f32[2048,512]{1,0:T(8,128)} fusion(bf16[2048,512]{1,0:T(8,128)(2,1)} %reshape.209, bf16[3,3,512,512]{3,2,1,0:T(8,128)(2,1)} %get-tuple-element.72), kind=kOutput, calls=%fused_computation.134 | convolution fusion | flops 1073741824 | bytes 6815744 | tf_op jit(solution)/shard_map/dot_general | solution.py:83
  294.8 3.4 fusion.68
  301.4 3.3 fusion.71
  304.7 21.2 %fusion.19 = (f32[2048]{0:T(1024)S(1)}, bf16[2048,512]{1,0:T(8,128)(2,1)}, f32[2048,512]{1,0:T(8,128)}, f32[2048,512]{1,0:T(8,128)}) fusion(bf16[2048,512]{1,0:T(8,128)(2,1)} %copy-done.18, f32[2048,512]{1,0:T(8,128)} %fusion.65, bf16[2048,512]{1,0:T(8,128)(2,1)} %reshape.208, bf16[3,3,512,512]{3,2,1,0:T(8,128)(2,1)S(1)} %bitcast.165, ...), kind=kOutput, calls=%fused_computation.32 | convolution fusion | flops 1155528704 | bytes 48766976 | tf_op jit(solution)/shard_map/dot_general | solution.py:83
  326.3 5.2 %mul.99 = f32[16,32,4,512]{3,2,1,0:T(4,128)} reshape(f32[2048,512]{1,0:T(8,128)} %get-tuple-element.75) | data formatting | bytes 8388608 | tf_op jit(solution)/shard_map/mul | solution.py:101
  331.6 5.2 %mul.101 = f32[16,32,4,512]{3,2,1,0:T(4,128)} reshape(f32[2048,512]{1,0:T(8,128)} %get-tuple-element.76) | data formatting | bytes 8388608 | tf_op jit(solution)/shard_map/mul | solution.py:101
  336.7 14.1 %fusion.17 = (bf16[16,32,4,512]{3,1,2,0:T(8,128)(2,1)S(1)}, bf16[16,32,4,512]{3,1,2,0:T(8,128)(2,1)}) fusion(f32[16,32,4]{1,2,0:T(4,128)S(1)} %copy.307, f32[32]{0:T(128)S(1)} %cosine_add_fusion, f32[16,32,4,512]{3,2,1,0:T(4,128)} %mul.101, f32[16,32,4,512]{3,2,1,0:T(4,128)} %mul.99, f32[16,32,4,512]{3,2,1,0:T(4,128)} %reshape.218), kind=kLoop, calls=%fused_computation.30 | loop fusion | flops 70254592 | bytes 16785536 | tf_op jit(solution)/shard_map/convert_element_type | solution.py:92
  350.9 7.2 %collective-permute-start.10 = (bf16[1,32,4,512]{3,1,2,0:T(8,128)(2,1)S(1)}, bf16[1,32,4,512]{3,1,2,0:T(8,128)(2,1)S(1)}, u32[]{:S(2)}, u32[]{:S(2)}) collective-permute-start(bf16[1,32,4,512]{3,1,2,0:T(8,128)(2,1)S(1)} %get-tuple-element.100), channel_id=1, source_target_pairs={{4,0},{8,4},{12,8},{16,12},{20,16},{24,20},{28,24},{32,28},{36,32}... | collective-permute-start | bytes 393224 | tf_op jit(solution)/shard_map/ppermute | solution.py:24
  358.1 3.9 fusion.52
  362.3 3.9 collective-permute-start.12
  368.3 3.4 collective-permute-start.11
  376.5 4.4 reshape.211
  380.9 5.1 %fusion.63 = f32[2048,512]{1,0:T(8,128)} fusion(bf16[2048,512]{1,0:T(8,128)(2,1)} %reshape.211, bf16[3,3,512,512]{3,2,1,0:T(8,128)(2,1)} %get-tuple-element.71), kind=kOutput, calls=%fused_computation.130 | convolution fusion | flops 1073741824 | bytes 6815744 | tf_op jit(solution)/shard_map/dot_general | solution.py:83
  389.0 4.0 reshape.216
  405.0 4.5 fusion.64
  415.3 4.4 fusion.59
  425.4 4.4 fusion.61
  429.8 3.4 fusion.77
  438.9 4.4 fusion.62
  449.1 4.5 fusion.58
  459.3 4.4 fusion.60
  463.7 15.6 %negate_multiply_fusion = (f32[2048,512]{1,0:T(8,128)}, f32[2048,512]{1,0:T(8,128)}) fusion(f32[2048,512]{1,0:T(8,128)} %fusion.58, bf16[2048,512]{1,0:T(8,128)(2,1)} %reshape.216, bf16[3,3,512,512]{3,2,1,0:T(8,128)(2,1)} %get-tuple-element.71, f32[2048,512]{1,0:T(8,128)} %fusion.59, f32[2048,512]{1,0:T(8,128)} %fusion.60, f32[2048,512]{1,0:T(8,128)} %fusion.52, ...), kind=kOutput, calls=%fused_computation.59 | convolution fusion | flops 1085276160 | bytes 44564480 | tf_op jit(solution)/shard_map/dot_general | solution.py:83
  479.3 5.2 %mul.110 = f32[16,32,4,512]{3,2,1,0:T(4,128)} reshape(f32[2048,512]{1,0:T(8,128)} %get-tuple-element.73) | data formatting | bytes 8388608 | tf_op jit(solution)/shard_map/mul | solution.py:101
  484.6 5.3 %mul.108 = f32[16,32,4,512]{3,2,1,0:T(4,128)} reshape(f32[2048,512]{1,0:T(8,128)} %get-tuple-element.74) | data formatting | bytes 8388608 | tf_op jit(solution)/shard_map/mul | solution.py:101
  489.9 11.4 %fusion.18 = bf16[16,32,4,512]{3,1,2,0:T(8,128)(2,1)S(1)} fusion(bf16[16,32,4,512]{3,1,2,0:T(8,128)(2,1)S(1)} %copy-done.13, f32[16,32,4,512]{3,2,1,0:T(4,128)} %mul.108, f32[16,32,4,512]{3,2,1,0:T(4,128)} %mul.110), kind=kLoop, calls=%fused_computation.31 | loop fusion | flops 67108864 | bytes 12582912 | tf_op jit(solution)/shard_map/convert_element_type | solution.py:101
  (220 shorter events, 190.1 us)
Async XLA Ops:
  0.0 185.1 %copy-start = (bf16[512,512]{1,0:T(8,128)(2,1)S(1)}, bf16[512,512]{1,0:T(8,128)(2,1)}, u32[]{:S(2)}) copy-start(bf16[512,512]{1,0:T(8,128)(2,1)} %param.22) | copy-start | bytes 1572868
  8.9 11.6 %copy-start.21 = (bf16[4,512]{1,0:T(4,128)(2,1)S(1)}, bf16[4,512]{1,0:T(4,128)(2,1)}, u32[]{:S(2)}) copy-start(bf16[4,512]{1,0:T(4,128)(2,1)} %param.16) | copy-start | bytes 12292
  8.9 11.6 %copy-start.20 = (bf16[16,32,512]{2,1,0:T(8,128)(2,1)S(1)}, bf16[16,32,512]{2,1,0:T(8,128)(2,1)}, u32[]{:S(2)}) copy-start(bf16[16,32,512]{2,1,0:T(8,128)(2,1)} %param.15) | copy-start | bytes 1572868
  8.9 14.9 %copy-start.22 = (s32[1,3,3]{2,0,1:T(1,128)S(1)}, s32[1,3,3]{2,0,1:T(1,128)}, u32[]{:S(2)}) copy-start(s32[1,3,3]{2,0,1:T(1,128)} %param.18) | copy-start | bytes 112
  11.4 23.6 %collective-permute-start.1 = (bf16[3,128,512]{2,1,0:T(8,128)(2,1)}, bf16[3,128,512]{2,1,0:T(8,128)(2,1)}, u32[]{:S(2)}, u32[]{:S(2)}) collective-permute-start(bf16[3,128,512]{2,1,0:T(8,128)(2,1)} %bitcast.8), channel_id=1, source_target_pairs={{0,124},{4,0},{8,4},{12,8},{16,12},{20,16},{24,20},{28,24},{32,28}... | collective-permute-start | bytes 1179656 | tf_op jit(solution)/shard_map/ppermute | solution.py:32
  20.5 15.7 %collective-permute-start = (bf16[3,128,512]{2,1,0:T(8,128)(2,1)}, bf16[3,128,512]{2,1,0:T(8,128)(2,1)}, u32[]{:S(2)}, u32[]{:S(2)}) collective-permute-start(bf16[3,128,512]{2,1,0:T(8,128)(2,1)} %bitcast.4), channel_id=1, source_target_pairs={{0,4},{4,8},{8,12},{12,16},{16,20},{20,24},{24,28},{28,32},{32,36}... | collective-permute-start | bytes 1179656 | tf_op jit(solution)/shard_map/ppermute | solution.py:32
  37.5 14.9 %collective-permute-start.2 = (bf16[3,128,512]{2,1,0:T(8,128)(2,1)S(1)}, bf16[3,128,512]{2,1,0:T(8,128)(2,1)S(1)}, u32[]{:S(2)}, u32[]{:S(2)}) collective-permute-start(bf16[3,128,512]{2,1,0:T(8,128)(2,1)S(1)} %get-tuple-element.105), channel_id=1, source_target_pairs={{0,1},{1,2},{2,3},{4,5},{5,6},{6,7},{8,9},{9,10},{10,11},{12,13},{... | collective-permute-start | bytes 1179656 | tf_op jit(solution)/shard_map/ppermute | solution.py:38
  42.0 10.6 %copy-start.23 = (bf16[512,512]{1,0:T(8,128)(2,1)S(1)}, bf16[512,512]{1,0:T(8,128)(2,1)}, u32[]{:S(2)}) copy-start(bf16[512,512]{1,0:T(8,128)(2,1)} %param.21) | copy-start | bytes 1572868
  42.0 10.5 %collective-permute-start.3 = (bf16[3,128,512]{2,1,0:T(8,128)(2,1)S(1)}, bf16[3,128,512]{2,1,0:T(8,128)(2,1)S(1)}, u32[]{:S(2)}, u32[]{:S(2)}) collective-permute-start(bf16[3,128,512]{2,1,0:T(8,128)(2,1)S(1)} %get-tuple-element.106), channel_id=1, source_target_pairs={{1,0},{2,1},{3,2},{5,4},{6,5},{7,6},{9,8},{10,9},{11,10},{13,12},{... | collective-permute-start | bytes 1179656 | tf_op jit(solution)/shard_map/ppermute | solution.py:38
  52.4 1.1 copy-start.24
  188.8 1.3 copy-start.18
  193.1 11.1 %copy-start.19 = (bf16[2048,512]{1,0:T(8,128)(2,1)S(1)}, bf16[2048,512]{1,0:T(8,128)(2,1)}, u32[]{:S(2)}) copy-start(bf16[2048,512]{1,0:T(8,128)(2,1)} %copy-done.18) | copy-start | bytes 6291460
  196.8 11.4 %collective-permute-start.4 = (bf16[1,32,4,512]{3,1,2,0:T(8,128)(2,1)S(1)}, bf16[1,32,4,512]{3,1,2,0:T(8,128)(2,1)S(1)}, u32[]{:S(2)}, u32[]{:S(2)}) collective-permute-start(bf16[1,32,4,512]{3,1,2,0:T(8,128)(2,1)S(1)} %get-tuple-element.103), channel_id=1, source_target_pairs={{0,4},{4,8},{8,12},{12,16},{16,20},{20,24},{24,28},{28,32},{32,36}... | collective-permute-start | bytes 393224 | tf_op jit(solution)/shard_map/ppermute | solution.py:21
  196.9 11.4 %collective-permute-start.5 = (bf16[1,32,4,512]{3,1,2,0:T(8,128)(2,1)S(1)}, bf16[1,32,4,512]{3,1,2,0:T(8,128)(2,1)S(1)}, u32[]{:S(2)}, u32[]{:S(2)}) collective-permute-start(bf16[1,32,4,512]{3,1,2,0:T(8,128)(2,1)S(1)} %get-tuple-element.104), channel_id=1, source_target_pairs={{4,0},{8,4},{12,8},{16,12},{20,16},{24,20},{28,24},{32,28},{36,32}... | collective-permute-start | bytes 393224 | tf_op jit(solution)/shard_map/ppermute | solution.py:24
  208.5 28.2 %collective-permute-start.7 = (bf16[18,1,4,512]{3,1,2,0:T(2,128)(2,1)S(1)}, bf16[18,1,4,512]{3,1,2,0:T(2,128)(2,1)S(1)}, u32[]{:S(2)}, u32[]{:S(2)}) collective-permute-start(bf16[18,1,4,512]{3,1,2,0:T(2,128)(2,1)S(1)} %get-tuple-element.95), channel_id=1, source_target_pairs={{0,1},{1,2},{2,3},{4,5},{5,6},{6,7},{8,9},{9,10},{10,11},{12,13},{... | collective-permute-start | bytes 221192 | tf_op jit(solution)/shard_map/ppermute | solution.py:21
  212.8 24.1 %collective-permute-start.8 = (bf16[18,1,4,512]{3,1,2,0:T(2,128)(2,1)S(1)}, bf16[18,1,4,512]{3,1,2,0:T(2,128)(2,1)S(1)}, u32[]{:S(2)}, u32[]{:S(2)}) collective-permute-start(bf16[18,1,4,512]{3,1,2,0:T(2,128)(2,1)S(1)} %get-tuple-element.96), channel_id=1, source_target_pairs={{1,0},{2,1},{3,2},{5,4},{6,5},{7,6},{9,8},{10,9},{11,10},{13,12},{... | collective-permute-start | bytes 221192 | tf_op jit(solution)/shard_map/ppermute | solution.py:24
  214.8 21.8 %collective-permute-start.6 = (bf16[2,18,4,512]{3,2,1,0:T(4,128)(2,1)S(1)}, bf16[2,18,4,512]{3,2,1,0:T(4,128)(2,1)S(1)}, u32[]{:S(2)}, u32[]{:S(2)}) collective-permute-start(bf16[2,18,4,512]{3,2,1,0:T(4,128)(2,1)S(1)} %pad_maximum_fusion.14), channel_id=1, source_target_pairs={{0,64},{4,68},{8,72},{12,76},{16,80},{20,84},{24,88},{28,92},{32,9... | collective-permute-start | bytes 442376 | tf_op jit(solution)/shard_map/ppermute | solution.py:32
  224.5 5.1 %copy-start.11 = (bf16[16,32,4,512]{3,1,2,0:T(8,128)(2,1)S(1)}, bf16[16,32,4,512]{3,1,2,0:T(8,128)(2,1)}, u32[]{:S(2)}) copy-start(bf16[16,32,4,512]{3,1,2,0:T(8,128)(2,1)} %get-tuple-element.101) | copy-start | bytes 6291460
  252.3 9.3 %copy-start.3 = (bf16[18,33,4,512]{3,1,2,0:T(8,128)(2,1)S(1)}, bf16[18,33,4,512]{3,1,2,0:T(8,128)(2,1)}, u32[]{:S(2)}) copy-start(bf16[18,33,4,512]{3,1,2,0:T(8,128)(2,1)} %get-tuple-element.94) | copy-start | bytes 7299076
  279.0 9.3 %slice-start = ((s8[4718592]{0:T(1024)(128)(4,1)}), s8[524288]{0:T(1024)(128)(4,1)S(1)}, s32[]{:S(2)}) async-start(s8[4718592]{0:T(1024)(128)(4,1)} %bitcast.164), calls=%async_computation | async-start | bytes 1048576
  283.2 5.1 %slice-start.1 = ((s8[4718592]{0:T(1024)(128)(4,1)}), s8[4194304]{0:T(1024)(128)(4,1)S(1)}, s32[]{:S(2)}) async-start(s8[4718592]{0:T(1024)(128)(4,1)} %bitcast.164), calls=%async_computation.1 | async-start | bytes 8388608
  283.2 5.1 %copy-start.7 = (bf16[2048,512]{1,0:T(8,128)(2,1)S(1)}, bf16[2048,512]{1,0:T(8,128)(2,1)}, u32[]{:S(2)}) copy-start(bf16[2048,512]{1,0:T(8,128)(2,1)} %reshape.207) | copy-start | bytes 6291460
  288.4 3.2 copy-start.10
  291.6 3.2 copy-start.8
  294.8 3.4 copy-start.9
  298.2 3.2 copy-start.6
  336.7 21.3 %copy-start.25 = (bf16[2048,512]{1,0:T(8,128)(2,1)S(1)}, bf16[2048,512]{1,0:T(8,128)(2,1)}, u32[]{:S(2)}) copy-start(bf16[2048,512]{1,0:T(8,128)(2,1)} %get-tuple-element.68) | copy-start | bytes 6291460
  350.8 11.2 %collective-permute-start.9 = (bf16[1,32,4,512]{3,1,2,0:T(8,128)(2,1)S(1)}, bf16[1,32,4,512]{3,1,2,0:T(8,128)(2,1)S(1)}, u32[]{:S(2)}, u32[]{:S(2)}) collective-permute-start(bf16[1,32,4,512]{3,1,2,0:T(8,128)(2,1)S(1)} %get-tuple-element.99), channel_id=1, source_target_pairs={{0,4},{4,8},{8,12},{12,16},{16,20},{20,24},{24,28},{28,32},{32,36}... | collective-permute-start | bytes 393224 | tf_op jit(solution)/shard_map/ppermute | solution.py:21
  350.9 11.1 %collective-permute-start.10 = (bf16[1,32,4,512]{3,1,2,0:T(8,128)(2,1)S(1)}, bf16[1,32,4,512]{3,1,2,0:T(8,128)(2,1)S(1)}, u32[]{:S(2)}, u32[]{:S(2)}) collective-permute-start(bf16[1,32,4,512]{3,1,2,0:T(8,128)(2,1)S(1)} %get-tuple-element.100), channel_id=1, source_target_pairs={{4,0},{8,4},{12,8},{16,12},{20,16},{24,20},{28,24},{32,28},{36,32}... | collective-permute-start | bytes 393224 | tf_op jit(solution)/shard_map/ppermute | solution.py:24
  362.3 30.8 %collective-permute-start.12 = (bf16[18,1,4,512]{3,1,2,0:T(2,128)(2,1)S(1)}, bf16[18,1,4,512]{3,1,2,0:T(2,128)(2,1)S(1)}, u32[]{:S(2)}, u32[]{:S(2)}) collective-permute-start(bf16[18,1,4,512]{3,1,2,0:T(2,128)(2,1)S(1)} %get-tuple-element.91), channel_id=1, source_target_pairs={{0,1},{1,2},{2,3},{4,5},{5,6},{6,7},{8,9},{9,10},{10,11},{12,13},{... | collective-permute-start | bytes 221192 | tf_op jit(solution)/shard_map/ppermute | solution.py:21
  366.2 27.1 %collective-permute-start.13 = (bf16[18,1,4,512]{3,1,2,0:T(2,128)(2,1)S(1)}, bf16[18,1,4,512]{3,1,2,0:T(2,128)(2,1)S(1)}, u32[]{:S(2)}, u32[]{:S(2)}) collective-permute-start(bf16[18,1,4,512]{3,1,2,0:T(2,128)(2,1)S(1)} %get-tuple-element.92), channel_id=1, source_target_pairs={{1,0},{2,1},{3,2},{5,4},{6,5},{7,6},{9,8},{10,9},{11,10},{13,12},{... | collective-permute-start | bytes 221192 | tf_op jit(solution)/shard_map/ppermute | solution.py:24
  368.3 24.7 %collective-permute-start.11 = (bf16[2,18,4,512]{3,2,1,0:T(4,128)(2,1)S(1)}, bf16[2,18,4,512]{3,2,1,0:T(4,128)(2,1)S(1)}, u32[]{:S(2)}, u32[]{:S(2)}) collective-permute-start(bf16[2,18,4,512]{3,2,1,0:T(4,128)(2,1)S(1)} %pad_maximum_fusion.15), channel_id=1, source_target_pairs={{0,64},{4,68},{8,72},{12,76},{16,80},{20,84},{24,88},{28,92},{32,9... | collective-permute-start | bytes 442376 | tf_op jit(solution)/shard_map/ppermute | solution.py:32
  380.9 5.1 %copy-start.12 = (bf16[16,32,4,512]{3,1,2,0:T(8,128)(2,1)S(1)}, bf16[16,32,4,512]{3,1,2,0:T(8,128)(2,1)}, u32[]{:S(2)}) copy-start(bf16[16,32,4,512]{3,1,2,0:T(8,128)(2,1)} %get-tuple-element.97) | copy-start | bytes 6291460
  404.9 4.6 copy-start.16
  415.3 4.5 copy-start.14
  425.4 4.4 copy-start.2
  438.8 4.5 copy-start.17
  449.1 4.5 copy-start.15
  459.3 4.4 copy-start.4
  459.3 4.4 copy-start.5
  484.6 5.3 %copy-start.13 = (bf16[16,32,4,512]{3,1,2,0:T(8,128)(2,1)S(1)}, bf16[16,32,4,512]{3,1,2,0:T(8,128)(2,1)}, u32[]{:S(2)}) copy-start(bf16[16,32,4,512]{3,1,2,0:T(8,128)(2,1)} %get-tuple-element.66) | copy-start | bytes 6291460
  489.9 14.5 %copy-start.1 = (bf16[512,512]{1,0:T(8,128)(2,1)S(1)}, bf16[512,512]{1,0:T(8,128)(2,1)}, u32[]{:S(2)}) copy-start(bf16[512,512]{1,0:T(8,128)(2,1)} %param.22) | copy-start | bytes 1572868
where the time goes:
time: 512 us; the launch traced here: 505 us
  matrix products  212 us (41%)
  local copies, waits for them, and re-layouts  170 us (33%)
  other arithmetic  73.2 us (14%)
  starting transfers between devices  46.6 us (9%)
    dot_general x18, matrix products, conv_taps(): jnp.dot(window, kernels[row_off, col_off], preferred_element_type=jnp.flo...  103 us
    slice x20, local copies, waits for them, and re-layouts, conv_taps(): padded[row_off:row_off + cells_lon, col_off:col_off + cells_lat]  63.1 us
    dot_general x16, matrix products, one_head(): jnp.dot(probs, v_part, preferred_element_type=jnp.float32)  53.1 us
    reshape x16, local copies, waits for them, and re-layouts, conv_taps(): padded[row_off:row_off + cells_lon, col_off:col_off + cells_lat]  48.9 us
    dot_general x16, matrix products, one_head(): lax.dot_general(q_part, k_part, (((1,), (1,)), ((), ())), preferred_eleme...  47.4 us
    reduce_sum x16, other arithmetic, one_head(): jnp.sum(weights, axis=1, keepdims=True)  21.7 us
    mul x4, local copies, waits for them, and re-layouts, conv_layer(): return (values + jax.nn.gelu(conv, approximate=False)).astype(jnp.bfloat16)  21 us
    ppermute x4, starting transfers between devices, with_halo(): lax.ppermute(lax.slice_in_dim(block, 0, width, axis=dim), axis, backward)  18.4 us
  transfers between devices with their start and end apart: 14, of which 1 were waited for; matrix products, arithmetic and copies ran while one was open for 15% of the time, Pallas kernels for 0%

commit v1 on v0

v1 whole, which is shorter than its diff:
```python
import functools
import math

import jax
import jax.numpy as jnp
from jax import lax
from jax.experimental import pallas as pl
from jax.experimental.pallas import tpu as pltpu
from jax.sharding import PartitionSpec as P

D = 512
HEADS = 16
HEAD = 32
CAP = 128
LON = 16
LAT = 32
CELLS = LON * LAT
LEVELS = 4
KEYS = 9 * CAP
SCALE = 1.0 / math.sqrt(HEAD)
LOG2E = 1.4426950408889634
CALM = 90.0
F32 = jnp.float32
BF16 = jnp.bfloat16
MIB = 1024 * 1024
NT = (((1,), (1,)), ((), ()))
TN = (((0,), (0,)), ((), ()))
AXES = ("lon", "lat")


def dot(a, b, dims=(((1,), (0,)), ((), ()))):
    return lax.dot_general(a, b, dims, preferred_element_type=F32)


def iota(shape, dim):
    return lax.broadcasted_iota(jnp.int32, shape, dim)


def gather_kernel(lat_ref, rows_ref, embed_ref, index_ref, out_ref, held):
    odd = lax.rem(lat_ref[0], 2)
    for s in range(4):
        part = rows_ref[s * 512 : (s + 1) * 512, :].astype(F32)
        held[s * 512 : (s + 1) * 512, :] = (part + embed_ref[s : s + 1, :].astype(F32)).astype(BF16)
    lanes = iota((CAP, 2048), 1)
    for a in range(3):
        picks = []
        for slot in range(3):
            if slot == 2:
                want = index_ref[0, a, 1:2, :]
            else:
                low, high = index_ref[0, a, 0:1, :], index_ref[0, a, 2:3, :]
                even_pick, odd_pick = (high, low) if slot == 0 else (low, high)
                want = jnp.where(odd == 1, odd_pick, even_pick)
            column = jnp.broadcast_to(want, (CAP, CAP)).T[:, 0:1]
            picks.append((lanes == column).astype(F32).astype(BF16))
        onehot = jnp.concatenate(picks, axis=0)
        out_ref[a] = dot(onehot, held[...]).astype(BF16).reshape(3, CAP, D)


def gather(lat, patch_rows, source_embed, margin_rows):
    return pl.pallas_call(
        gather_kernel,
        out_shape=jax.ShapeDtypeStruct((3, 3, CAP, D), BF16),
        in_specs=[
            pl.BlockSpec(memory_space=pltpu.SMEM),
            pl.BlockSpec(memory_space=pltpu.VMEM),
            pl.BlockSpec(memory_space=pltpu.VMEM),
            pl.BlockSpec(memory_space=pltpu.VMEM),
        ],
        out_specs=pl.BlockSpec(memory_space=pltpu.VMEM),
        scratch_shapes=[pltpu.VMEM((2048, D), BF16)],
        compiler_params=pltpu.CompilerParams(vmem_limit_bytes=40 * MIB),
        name="gather_rows",
    )(lat, patch_rows, source_embed, margin_rows)


def gain_of(lat, shape, dim):
    row = (lat * LAT + iota(shape, dim)).astype(F32)
    phi = (row + 0.5) / 128 * jnp.pi - jnp.pi / 2
    return 0.5 + jnp.cos(phi)


def normal(x, gain):
    spread = jnp.sqrt(jnp.mean(x * x, axis=-1, keepdims=True) + 1e-06)
    return x / spread * gain


def attend_kernel(
    lat_ref, count_ref, a0, a1, a2, a3, a4, a5, a6, a7, a8,
    cell_ref, level_ref, wq_ref, wk_ref, wv_ref, wo_ref,
    x_ref, k_s, v_s, q_s, att, live_col, live_row, ql_s,
):
    lists = (a0, a1, a2, a3, a4, a5, a6, a7, a8)
    for n, ref in enumerate(lists):
        span = slice(n * CAP, (n + 1) * CAP)
        rows = ref[...].reshape(CAP, D)
        k_s[span, :] = dot(rows, wk_ref[...]).astype(BF16)
        v_s[span, :] = dot(rows, wv_ref[...]).astype(BF16)
        live_col[span, :] = (iota((CAP, 128), 0) < count_ref[n]).astype(F32)
        live_row[:, span] = (iota((8, CAP), 1) < count_ref[n]).astype(F32)
    cells = cell_ref[...]
    level = jnp.concatenate([level_ref[...], level_ref[...]], axis=0)
    factor = SCALE * LOG2E
    qc = dot(cells, wq_ref[...]) * factor
    ql = dot(level, wq_ref[...]) * factor
    q_s[...] = qc.astype(BF16)
    ql_s[...] = ql
    heads = (iota((D, 128), 0) // HEAD == iota((D, 128), 1)).astype(F32).astype(BF16)

    def norms(values):
        return jnp.max(dot((values * values).astype(BF16), heads), axis=0, keepdims=True)

    keys_f = k_s[...].astype(F32)
    key_norm = norms(keys_f)
    bound = jnp.sqrt(norms(qc) * key_norm) + jnp.sqrt(norms(ql) * key_norm)
    calm = jnp.max(bound) < CALM
    group_lane = iota((1, 128), 1) // HEAD

    @pl.when(calm)
    def _():
        def group(hg, carry):
            lanes = pl.ds(pl.multiple_of(hg * 128, 128), 128)
            kg = k_s[:, lanes]
            vg = v_s[:, lanes]
            qg = q_s[:, lanes]
            lg = ql_s[:, lanes].astype(BF16)
            col = iota((8, 512), 1)
            pick = (col // HEAD % 4 - col // 128 + 4) % 4
            choose = ((iota((8, 512), 0) == pick) & (iota((8, 512), 0) < 4)).astype(F32).astype(BF16)
            spread = dot(lg, choose, TN)
            col2, row2 = iota((128, 512), 1), iota((128, 512), 0)
            own = row2 // HEAD == col2 // 128
            ql_block = jnp.where(own, spread, 0.0).astype(BF16)
            copies = (own & (row2 % HEAD == col2 % HEAD)).astype(F32).astype(BF16)
            level_exp = jnp.exp2(dot(kg, ql_block))
            vals = dot(vg, copies)
            live = live_col[...]
            kept = []
            for i in range(4):
                span = slice(i * 128, (i + 1) * 128)
                part = level_exp[:, span] * live
                weighted = jnp.concatenate([part * vals[:, span], part], axis=1).astype(BF16)
                km = jnp.where(group_lane == i, kg, jnp.zeros_like(kg))
                probs = jnp.exp2(dot(qg, km, NT)).astype(BF16)
                both = dot(probs, weighted)
                kept.append(both[:, :128] / both[:, 128:])
            for lev in range(LEVELS):
                z = kept[0]
                for i in range(4):
                    z = jnp.where(group_lane == (i + lev) % 4, kept[i], z)
                if lev:
                    z = pltpu.roll(z, 128 - HEAD * lev, axis=1)
                att[lev, :, lanes] = z.astype(BF16)
            return carry

        lax.fori_loop(0, 4, group, 0)

    @pl.when(jnp.logical_not(calm))
    def _():
        def one_level(lev, carry):
            four = level_ref[...].astype(F32)
            mine = jnp.sum(jnp.where(iota((LEVELS, D), 0) == lev, four, 0.0), axis=0, keepdims=True)
            latent = (cell_ref[...].astype(F32) + mine).astype(BF16)
            q_s[...] = dot(latent, wq_ref[...]).astype(BF16)

            def group(hg, carry):
                lanes = pl.ds(pl.multiple_of(hg * 128, 128), 128)
                kg = k_s[:, lanes]
                vg = v_s[:, lanes]
                qg = q_s[:, lanes]

                def head(i, total):
                    mine = group_lane == i
                    scores = dot(qg, jnp.where(mine, kg, jnp.zeros_like(kg)), NT) * SCALE
                    scores = jnp.where(live_row[0:1, :] > 0.5, scores, -1e30)
                    top = jnp.max(scores, axis=1, keepdims=True)
                    weights = jnp.exp(scores - top)
                    probs = (weights / jnp.sum(weights, axis=1, keepdims=True)).astype(BF16)
                    return total + dot(probs, jnp.where(mine, vg, jnp.zeros_like(vg)))

                total = lax.fori_loop(0, 4, head, jnp.zeros((CELLS, 128), F32))
                att[lev, :, lanes] = total.astype(BF16)
                return carry

            return lax.fori_loop(0, 4, group, carry)

        lax.fori_loop(0, LEVELS, one_level, 0)

    for lev in range(LEVELS):
        latent = (cell_ref[...].astype(F32) + level_ref[lev : lev + 1, :].astype(F32)).astype(BF16)
        x = (latent.astype(F32) + dot(att[lev], wo_ref[...])).astype(BF16)
        x_ref[lev] = x


def attend(lat, counts, lists, cells, level_query, wq, wk, wv, wo):
    vmem = pl.BlockSpec(memory_space=pltpu.VMEM)
    smem = pl.BlockSpec(memory_space=pltpu.SMEM)
    return pl.pallas_call(
        attend_kernel,
        out_shape=jax.ShapeDtypeStruct((LEVELS, CELLS, D), BF16),
        in_specs=[smem, smem] + [vmem] * 15,
        out_specs=vmem,
        scratch_shapes=[
            pltpu.VMEM((KEYS, D), BF16),
            pltpu.VMEM((KEYS, D), BF16),
            pltpu.VMEM((CELLS, D), BF16),
            pltpu.VMEM((LEVELS, CELLS, D), BF16),
            pltpu.VMEM((KEYS, 128), F32),
            pltpu.VMEM((8, KEYS), F32),
            pltpu.VMEM((8, D), F32),
        ],
        compiler_params=pltpu.CompilerParams(vmem_limit_bytes=56 * MIB),
        name="attend",
    )(lat, counts, *lists, cells, level_query, wq, wk, wv, wo)


def conv_kernel(lat_ref, x_ref, west_ref, east_ref, north_ref, south_ref, w_ref, out_ref, near):
    gain = gain_of(lat_ref[0], (LAT, D), 0)
    x = x_ref[0].astype(F32)
    u = normal(x, jnp.tile(gain, (LON, 1))).astype(BF16).astype(F32)
    wide = jnp.concatenate([west_ref[0].astype(F32), u, east_ref[0].astype(F32)], axis=0)
    count = (LON + 2) * LAT
    place = iota((LON + 2, LAT, D), 1)
    before = pltpu.roll(wide, 1, axis=0).reshape(LON + 2, LAT, D)
    after = pltpu.roll(wide, count - 1, axis=0).reshape(LON + 2, LAT, D)
    north = north_ref[0].astype(F32)[:, None, :]
    south = south_ref[0].astype(F32)[:, None, :]
    near[:, 0:512] = jnp.where(place == 0, north, before).astype(BF16).reshape(count, D)
    near[:, 512:1024] = wide.astype(BF16)
    near[:, 1024:1536] = jnp.where(place == LAT - 1, south, after).astype(BF16).reshape(count, D)
    total = dot(near[0:CELLS, :], w_ref[0])
    total += dot(near[LAT : LAT + CELLS, :], w_ref[1])
    total += dot(near[2 * LAT : 2 * LAT + CELLS, :], w_ref[2])
    gelu = 0.5 * total * (1.0 + lax.erf(total * (2.0 ** -0.5)))
    out_ref[0] = (x + gelu).astype(BF16)


def conv(lat, x, west, east, north, south, weight):
    per = lambda rows: pl.BlockSpec((1, rows, D), lambda i: (i, 0, 0))
    return pl.pallas_call(
        conv_kernel,
        grid=(LEVELS,),
        out_shape=jax.ShapeDtypeStruct((LEVELS, CELLS, D), BF16),
        in_specs=[
            pl.BlockSpec(memory_space=pltpu.SMEM),
            per(CELLS), per(LAT), per(LAT), per(LON + 2), per(LON + 2),
            pl.BlockSpec((3, 3 * D, D), lambda i: (0, 0, 0)),
        ],
        out_specs=per(CELLS),
        scratch_shapes=[pltpu.VMEM(((LON + 2) * LAT, 3 * D), BF16)],
        compiler_params=pltpu.CompilerParams(vmem_limit_bytes=56 * MIB),
        name="conv",
    )(lat, x, west, east, north, south, weight)


def route(target):
    pairs = []
    for lon in range(32):
        for lat in range(4):
            there = target(lon, lat)
            if there is not None:
                pairs.append((lon * 4 + lat, there[0] % 32 * 4 + there[1]))
    return pairs


EAST = route(lambda lon, lat: (lon + 1, lat))
WEST = route(lambda lon, lat: (lon - 1, lat))
FIRST = route(lambda lon, lat: (lon, lat ^ 1))
SECOND = route(lambda lon, lat: (lon + 16 if lat in (0, 3) else lon, (0, 2, 1, 3)[lat]))


def send(block, pairs):
    return lax.ppermute(block, AXES, pairs)


def edges(x, lat, lat_place):
    grid = x.reshape(LEVELS, LON, LAT, D)
    gain = 0.5 + jnp.cos((lat_place * LAT + jnp.arange(LAT)).astype(F32) * (jnp.pi / 128) + (0.5 * jnp.pi / 128 - jnp.pi / 2))

    def u(part, scale):
        return normal(part.astype(F32), scale).astype(BF16)

    first = u(grid[:, 0], gain[:, None])
    last = u(grid[:, LON - 1], gain[:, None])
    north = u(grid[:, :, 0], gain[0])
    south = u(grid[:, :, LAT - 1], gain[LAT - 1])
    return first, last, north, south


def halos(x, lat, lat_place):
    first, last, north, south = edges(x, lat, lat_place)
    west = send(last, EAST)
    east = send(first, WEST)
    north = jnp.concatenate([west[:, :1], north, east[:, :1]], axis=1)
    south = jnp.concatenate([west[:, -1:], south, east[:, -1:]], axis=1)
    odd = lat_place % 2 == 1
    one = send(jnp.where(odd, north, south), FIRST)
    two = send(jnp.where(odd, south, north), SECOND)
    return west, east, jnp.where(odd, one, two), jnp.where(odd, two, one)


def shards(
    patch_rows, source_embed, cell_embed, level_query, margin_rows, margin_counts,
    query_weight, key_weight, value_weight, out_weight, conv_weight,
):
    lat_place = lax.axis_index("lat")
    lat = lat_place.astype(jnp.int32).reshape(1)
    payload = gather(lat, patch_rows, source_embed, margin_rows)
    from_west = send(payload[2], EAST)
    from_east = send(payload[0], WEST)
    own = payload[1]
    one = send(jnp.stack([from_west[0], own[0], from_east[0]]), FIRST)
    two = send(jnp.stack([from_west[1], own[1], from_east[1]]), SECOND)
    lists = [from_west[2], own[2], from_east[2], one[0], one[1], one[2], two[0], two[1], two[2]]
    odd = lat_place % 2 == 1
    counts = margin_counts[0]
    first = jnp.where(odd, counts[:, 0], counts[:, 2])
    second = jnp.where(odd, counts[:, 2], counts[:, 0])
    counts = jnp.concatenate([counts[:, 1], first, second])
    x = attend(lat, counts, lists, cell_embed.reshape(CELLS, D), level_query,
               query_weight, key_weight, value_weight, out_weight)
    weight = conv_weight.reshape(2, 3, 3 * D, D)
    for layer in range(2):
        west, east, north, south = halos(x, lat, lat_place)
        x = conv(lat, x, west, east, north, south, weight[layer])
    return x.reshape(LEVELS, LON, LAT, D).transpose(1, 2, 0, 3)


def solution(mesh):
    placed = (
        P(AXES, None), P(), P("lon", "lat", None), P(), P(AXES, None, None, None), P(AXES, None, None),
        P(), P(), P(), P(), P(),
    )
    return jax.shard_map(
        shards, mesh=mesh, in_specs=placed, out_specs=P("lon", "lat", None, None), check_vma=False
    )
```

time: 512 us -> 254 us (0.50); the launches traced: 505 us -> 253 us
  matrix products: 212 us -> 0 us
  Pallas kernels: 0 us -> 160 us
  local copies, waits for them, and re-layouts: 170 us -> 23 us
  other arithmetic: 73.2 us -> 10.1 us
  waiting for transfers between devices: 1.21 us -> 38.9 us
  starting transfers between devices: 46.6 us -> 20.7 us
    dot_general x54 -> x0, matrix products: 212 us -> none  [the longest x18 103 us: conv_taps(): jnp.dot(window, kernels[row_off, col_off], preferred_element_type=jnp.flo...]
    pallas_call x0 -> x4, Pallas kernels: none -> 160 us  [the longest x1 127 us: attend(): pl.pallas_call(attend_kernel, out_shape=jax.ShapeDtypeStruct((LEVELS, CEL...]
    reshape x20 -> x1, local copies, waits for them, and re-layouts: 61.5 us -> 4.68 us  [shards(): return x.reshape(LEVELS, LON, LAT, D).transpose(1, 2, 0, 3)]
    slice x23 -> x11, local copies, waits for them, and re-layouts: 64.1 us -> 13.8 us  [the longest x1 8.22 us: shards(): x = conv(lat, x, west, east, north, south, weight[layer])]
    ppermute x14 -> x12, waiting for transfers between devices: 1.21 us -> 38.9 us  [send(): return lax.ppermute(block, AXES, pairs)]
    convert_element_type x8 -> x6, other arithmetic: 35.1 us -> 4.99 us  [u(): return normal(part.astype(F32), scale).astype(BF16)]
    ppermute x14 -> x12, starting transfers between devices: 46.6 us -> 20.7 us  [send(): return lax.ppermute(block, AXES, pairs)]
    mul x6 -> x0, local copies, waits for them, and re-layouts: 21.2 us -> none  [the longest x4 21 us: conv_layer(): return (values + jax.nn.gelu(conv, approximate=False)).astype(jnp.bfloat16)]
  transfers between devices with their start and end apart: 14 -> 12, of which waited for: 1 -> 9; matrix products, arithmetic and copies ran while one was open for 15% -> 6% of each run, Pallas kernels for 0% -> 0%
where the time goes in v1:
time: 254 us; the launch traced here: 253 us
  Pallas kernels  160 us (63%)
  waiting for transfers between devices  38.9 us (15%)
  local copies, waits for them, and re-layouts  23 us (9%)
  starting transfers between devices  20.7 us (8%)
  other arithmetic  10.1 us (4%)
    pallas_call x1, Pallas kernels, attend(): pl.pallas_call(attend_kernel, out_shape=jax.ShapeDtypeStruct((LEVELS, CEL...  127 us
    ppermute x12, waiting for transfers between devices, send(): return lax.ppermute(block, AXES, pairs)  38.9 us
    pallas_call x2, Pallas kernels, conv(): pl.pallas_call(conv_kernel, grid=(LEVELS,), out_shape=jax.ShapeDtypeStruc...  30.1 us
    ppermute x12, starting transfers between devices, send(): return lax.ppermute(block, AXES, pairs)  20.7 us
    slice x1, local copies, waits for them, and re-layouts, shards(): x = conv(lat, x, west, east, north, south, weight[layer])  8.22 us
  transfers between devices with their start and end apart: 12, of which 9 were waited for; matrix products, arithmetic and copies ran while one was open for 6% of the time, Pallas kernels for 0%

profile of v1, /device:TPU:1, one launch (start us, length us, event | category | flops | bytes accessed | tf_op | source)
XLA Modules:
  0.0 253.0 jit_solution(8174102147092096885)
XLA Ops:
  0.0 0.7 copy.51.index_ref
  0.7 1.6 copy-done
  2.3 0.7 copy-done.1
  3.0 2.9 %gather_rows.1 = bf16[3,3,128,512]{3,2,1,0:T(8,128)(2,1)S(1)} custom-call(s32[1]{0:T(128)} %bitcast.lat_ref, bf16[2048,512]{1,0:T(8,128)(2,1)S(1)} %copy-done, bf16[4,512]{1,0:T(4,128)(2,1)S(1)} %copy-done.1, s32[1,3,3,128]{3,2,1,0:T(4,128)S(1)} %copy.51.index_ref), custom_call_target="tpu_custom_call" | custom-call | tf_op jit(solution)/shard_map/gather_rows/pallas_call | solution.py:61
  5.9 0.1 slice_bitcast_fusion
  6.0 9.1 %collective-permute-start.1 = (bf16[3,128,512]{2,1,0:T(8,128)(2,1)S(1)}, bf16[3,128,512]{2,1,0:T(8,128)(2,1)S(1)}, u32[]{:S(2)}, u32[]{:S(2)}) collective-permute-start(bf16[3,128,512]{2,1,0:T(8,128)(2,1)S(1)} %get-tuple-element.25), channel_id=1, source_target_pairs={{0,124},{1,125},{2,126},{3,127},{4,0},{5,1},{6,2},{7,3},{8,4},{9,5... | collective-permute-start | bytes 1179656 | tf_op jit(solution)/shard_map/ppermute | solution.py:273
  15.1 0.0 collective-permute-start
  15.1 0.7 slice_bitcast_fusion.9
  15.8 0.0 copy-done.6
  15.8 0.2 slice_reduce_fusion
  16.0 6.9 %collective-permute-done.1 = bf16[3,128,512]{2,1,0:T(8,128)(2,1)S(1)} collective-permute-done((bf16[3,128,512]{2,1,0:T(8,128)(2,1)S(1)}, bf16[3,128,512]{2,1,0:T(8,128)(2,1)S(1)}, u32[]{:S(2)}, u32[]{:S(2)}) %collective-permute-start.1) | collective-permute-done | bytes 393248 | tf_op jit(solution)/shard_map/ppermute | solution.py:273
  22.9 0.7 fusion.28
  23.6 6.9 %collective-permute-done = bf16[3,128,512]{2,1,0:T(8,128)(2,1)S(1)} collective-permute-done((bf16[3,128,512]{2,1,0:T(8,128)(2,1)S(1)}, bf16[3,128,512]{2,1,0:T(8,128)(2,1)S(1)}, u32[]{:S(2)}, u32[]{:S(2)}) %collective-permute-start) | collective-permute-done | bytes 393248 | tf_op jit(solution)/shard_map/ppermute | solution.py:273
  30.5 0.7 fusion.27
  31.2 1.9 collective-permute-start.2
  33.3 0.7 collective-permute-start.3
  34.0 0.6 pad_add_fusion.count_ref
  34.6 0.6 fusion.33
  35.2 0.0 collective-permute-done.2
  35.2 0.8 slice_bitcast_fusion.10
  36.0 8.0 %collective-permute-done.3 = bf16[3,128,512]{2,1,0:T(8,128)(2,1)S(1)} collective-permute-done((bf16[3,128,512]{2,1,0:T(8,128)(2,1)S(1)}, bf16[3,128,512]{2,1,0:T(8,128)(2,1)S(1)}, u32[]{:S(2)}, u32[]{:S(2)}) %collective-permute-start.3) | collective-permute-done | bytes 393248 | tf_op jit(solution)/shard_map/ppermute | solution.py:273
  44.0 0.8 slice_bitcast_fusion.6
  44.8 127.1 %attend.1.x_ref = bf16[4,512,512]{2,1,0:T(8,128)(2,1)} custom-call(s32[1]{0:T(128)} %bitcast.lat_ref, s32[9]{0:T(128)} %pad_add_fusion.count_ref, bf16[128,512]{1,0:T(8,128)(2,1)} %get-tuple-element.32.a0, bf16[128,512]{1,0:T(8,128)(2,1)} %get-tuple-element.24.a1, bf16[128,512]{1,0:T(8,128)(2,1)} %get-tuple-element.35.a2, ...), custom_call_target="tpu_custom_call" | custom-call | tf_op jit(solution)/shard_map/attend/pallas_call | solution.py:198
  171.9 1.1 fusion.3
  173.0 1.4 fusion.26
  174.4 1.1 fusion.5
  175.5 1.1 collective-permute-start.5
  176.6 0.5 collective-permute-start.4
  177.1 0.1 fusion.12
  177.2 0.6 fusion.14
  177.9 0.7 fusion.17
  178.6 1.0 collective-permute-done.5.east_ref
  179.6 7.6 %collective-permute-done.4.west_ref = bf16[4,32,512]{2,1,0:T(8,128)(2,1)S(1)} collective-permute-done((bf16[4,32,512]{2,1,0:T(8,128)(2,1)S(1)}, bf16[4,32,512]{2,1,0:T(8,128)(2,1)S(1)}, u32[]{:S(2)}, u32[]{:S(2)}) %collective-permute-start.4) | collective-permute-done | bytes 131104 | tf_op jit(solution)/shard_map/ppermute | solution.py:273
  187.2 0.1 broadcast_select_fusion.6
  187.3 0.8 collective-permute-start.7
  188.1 1.1 collective-permute-start.6
  189.2 8.2 %fusion.24 = (bf16[1,3,3,512,512]{4,3,2,1,0:T(8,128)(2,1)}, bf16[1,3,3,512,512]{4,3,2,1,0:T(8,128)(2,1)}) fusion(bf16[2,3,3,512,512]{4,3,2,1,0:T(8,128)(2,1)} %param.21), kind=kLoop, calls=%fused_computation.90 | loop fusion | bytes 18874368 | tf_op jit(solution)/shard_map/slice | solution.py:325
  197.5 0.0 copy-done.2
  197.5 0.0 copy-done.4
  197.5 0.0 collective-permute-done.7
  197.5 0.0 collective-permute-done.6
  197.5 0.7 broadcast_select_fusion.4
  198.2 15.0 %conv.2.x_ref = bf16[4,512,512]{2,1,0:T(8,128)(2,1)} custom-call(s32[1]{0:T(128)} %bitcast.lat_ref, bf16[4,512,512]{2,1,0:T(8,128)(2,1)} %attend.1.x_ref, bf16[4,32,512]{2,1,0:T(8,128)(2,1)} %copy-done.4, bf16[4,32,512]{2,1,0:T(8,128)(2,1)} %copy-done.2, bf16[4,18,512]{2,1,0:T(8,128)(2,1)} %get-tuple-element.42.north_ref, ...), custom_call_target="tpu_custom_call" | custom-call | tf_op jit(solution)/shard_map/conv/pallas_call | solution.py:240
  213.2 1.1 fusion.9
  214.3 1.4 fusion.25
  215.7 1.1 fusion.11
  216.9 0.1 collective-permute-start.9
  217.0 1.5 collective-permute-start.8
  218.4 0.1 fusion.18
  218.5 0.7 fusion.20
  219.2 0.1 fusion.21
  219.3 0.7 fusion.23
  220.0 2.0 collective-permute-done.9.east_ref
  222.1 5.6 %collective-permute-done.8.west_ref = bf16[4,32,512]{2,1,0:T(8,128)(2,1)S(1)} collective-permute-done((bf16[4,32,512]{2,1,0:T(8,128)(2,1)S(1)}, bf16[4,32,512]{2,1,0:T(8,128)(2,1)S(1)}, u32[]{:S(2)}, u32[]{:S(2)}) %collective-permute-start.8) | collective-permute-done | bytes 131104 | tf_op jit(solution)/shard_map/ppermute | solution.py:273
  227.6 0.1 broadcast_select_fusion.2
  227.7 1.0 collective-permute-start.11
  228.7 2.9 %collective-permute-start.10 = (bf16[4,18,512]{2,1,0:T(8,128)(2,1)S(1)}, bf16[4,18,512]{2,1,0:T(8,128)(2,1)S(1)}, u32[]{:S(2)}, u32[]{:S(2)}) collective-permute-start(bf16[4,18,512]{2,1,0:T(8,128)(2,1)S(1)} %get-tuple-element.44), channel_id=1, source_target_pairs={{0,1},{1,0},{2,3},{3,2},{4,5},{5,4},{6,7},{7,6},{8,9},{9,8},{10,11... | collective-permute-start | bytes 221192 | tf_op jit(solution)/shard_map/ppermute | solution.py:273
  231.6 0.2 collective-permute-done.11
  231.9 0.7 collective-permute-done.10
  232.6 0.7 broadcast_select_fusion
  233.3 0.0 copy-done.3
  233.3 0.0 copy-done.5
  233.3 15.1 %conv.3 = bf16[4,512,512]{2,1,0:T(8,128)(2,1)} custom-call(s32[1]{0:T(128)} %bitcast.lat_ref, bf16[4,512,512]{2,1,0:T(8,128)(2,1)} %conv.2.x_ref, bf16[4,32,512]{2,1,0:T(8,128)(2,1)} %copy-done.5, bf16[4,32,512]{2,1,0:T(8,128)(2,1)} %copy-done.3, bf16[4,18,512]{2,1,0:T(8,128)(2,1)} %get-tuple-element.40.north_ref, ...), custom_call_target="tpu_custom_call" | custom-call | tf_op jit(solution)/shard_map/conv/pallas_call | solution.py:240
  248.4 4.7 %copy.92 = bf16[4,16,32,512]{3,0,2,1:T(4,128)(2,1)} copy(bf16[4,16,32,512]{3,2,1,0:T(8,128)(2,1)} %bitcast.113) | data formatting | bytes 4194304 | tf_op jit(solution)/shard_map/reshape | solution.py:326
  (22 shorter events, 0.3 us)
Async XLA Ops:
  0.7 1.6 copy-start
  2.3 0.7 copy-start.1
  3.0 12.8 %copy-start.6 = (s32[1,3,3]{2,0,1:T(1,128)S(1)}, s32[1,3,3]{2,0,1:T(1,128)}, u32[]{:S(2)}) copy-start(s32[1,3,3]{2,0,1:T(1,128)} %param.16) | copy-start | bytes 112
  6.0 16.9 %collective-permute-start.1 = (bf16[3,128,512]{2,1,0:T(8,128)(2,1)S(1)}, bf16[3,128,512]{2,1,0:T(8,128)(2,1)S(1)}, u32[]{:S(2)}, u32[]{:S(2)}) collective-permute-start(bf16[3,128,512]{2,1,0:T(8,128)(2,1)S(1)} %get-tuple-element.25), channel_id=1, source_target_pairs={{0,124},{1,125},{2,126},{3,127},{4,0},{5,1},{6,2},{7,3},{8,4},{9,5... | collective-permute-start | bytes 1179656 | tf_op jit(solution)/shard_map/ppermute | solution.py:273
  15.1 15.4 %collective-permute-start = (bf16[3,128,512]{2,1,0:T(8,128)(2,1)S(1)}, bf16[3,128,512]{2,1,0:T(8,128)(2,1)S(1)}, u32[]{:S(2)}, u32[]{:S(2)}) collective-permute-start(bf16[3,128,512]{2,1,0:T(8,128)(2,1)S(1)} %get-tuple-element.26), channel_id=1, source_target_pairs={{0,4},{1,5},{2,6},{3,7},{4,8},{5,9},{6,10},{7,11},{8,12},{9,13},{1... | collective-permute-start | bytes 1179656 | tf_op jit(solution)/shard_map/ppermute | solution.py:273
  31.2 4.0 %collective-permute-start.2 = (bf16[3,128,512]{2,1,0:T(8,128)(2,1)S(1)}, bf16[3,128,512]{2,1,0:T(8,128)(2,1)S(1)}, u32[]{:S(2)}, u32[]{:S(2)}) collective-permute-start(bf16[3,128,512]{2,1,0:T(8,128)(2,1)S(1)} %pad_maximum_fusion), channel_id=1, source_target_pairs={{0,1},{1,0},{2,3},{3,2},{4,5},{5,4},{6,7},{7,6},{8,9},{9,8},{10,11... | collective-permute-start | bytes 1179656 | tf_op jit(solution)/shard_map/ppermute | solution.py:273
  33.3 10.8 %collective-permute-start.3 = (bf16[3,128,512]{2,1,0:T(8,128)(2,1)S(1)}, bf16[3,128,512]{2,1,0:T(8,128)(2,1)S(1)}, u32[]{:S(2)}, u32[]{:S(2)}) collective-permute-start(bf16[3,128,512]{2,1,0:T(8,128)(2,1)S(1)} %pad_maximum_fusion.1), channel_id=1, source_target_pairs={{0,64},{1,2},{2,1},{3,67},{4,68},{5,6},{6,5},{7,71},{8,72},{9,10},... | collective-permute-start | bytes 1179656 | tf_op jit(solution)/shard_map/ppermute | solution.py:273
  175.5 4.0 %collective-permute-start.5 = (bf16[4,32,512]{2,1,0:T(8,128)(2,1)S(1)}, bf16[4,32,512]{2,1,0:T(8,128)(2,1)S(1)}, u32[]{:S(2)}, u32[]{:S(2)}) collective-permute-start(bf16[4,32,512]{2,1,0:T(8,128)(2,1)S(1)} %get-tuple-element.16), channel_id=1, source_target_pairs={{0,124},{1,125},{2,126},{3,127},{4,0},{5,1},{6,2},{7,3},{8,4},{9,5... | collective-permute-start | bytes 393224 | tf_op jit(solution)/shard_map/ppermute | solution.py:273
  176.6 10.5 %collective-permute-start.4 = (bf16[4,32,512]{2,1,0:T(8,128)(2,1)S(1)}, bf16[4,32,512]{2,1,0:T(8,128)(2,1)S(1)}, u32[]{:S(2)}, u32[]{:S(2)}) collective-permute-start(bf16[4,32,512]{2,1,0:T(8,128)(2,1)S(1)} %get-tuple-element.17), channel_id=1, source_target_pairs={{0,4},{1,5},{2,6},{3,7},{4,8},{5,9},{6,10},{7,11},{8,12},{9,13},{1... | collective-permute-start | bytes 393224 | tf_op jit(solution)/shard_map/ppermute | solution.py:273
  179.5 17.9 %copy-start.2 = (bf16[4,32,512]{2,1,0:T(8,128)(2,1)}, bf16[4,32,512]{2,1,0:T(8,128)(2,1)S(1)}, u32[]{:S(2)}) copy-start(bf16[4,32,512]{2,1,0:T(8,128)(2,1)S(1)} %collective-permute-done.5.east_ref) | copy-start | bytes 393220
  187.1 10.3 %copy-start.4 = (bf16[4,32,512]{2,1,0:T(8,128)(2,1)}, bf16[4,32,512]{2,1,0:T(8,128)(2,1)S(1)}, u32[]{:S(2)}) copy-start(bf16[4,32,512]{2,1,0:T(8,128)(2,1)S(1)} %collective-permute-done.4.west_ref) | copy-start | bytes 393220
  187.3 10.2 %collective-permute-start.7 = (bf16[4,18,512]{2,1,0:T(8,128)(2,1)S(1)}, bf16[4,18,512]{2,1,0:T(8,128)(2,1)S(1)}, u32[]{:S(2)}, u32[]{:S(2)}) collective-permute-start(bf16[4,18,512]{2,1,0:T(8,128)(2,1)S(1)} %get-tuple-element.45), channel_id=1, source_target_pairs={{0,64},{1,2},{2,1},{3,67},{4,68},{5,6},{6,5},{7,71},{8,72},{9,10},... | collective-permute-start | bytes 221192 | tf_op jit(solution)/shard_map/ppermute | solution.py:273
  188.1 9.4 %collective-permute-start.6 = (bf16[4,18,512]{2,1,0:T(8,128)(2,1)S(1)}, bf16[4,18,512]{2,1,0:T(8,128)(2,1)S(1)}, u32[]{:S(2)}, u32[]{:S(2)}) collective-permute-start(bf16[4,18,512]{2,1,0:T(8,128)(2,1)S(1)} %get-tuple-element.46), channel_id=1, source_target_pairs={{0,1},{1,0},{2,3},{3,2},{4,5},{5,4},{6,7},{7,6},{8,9},{9,8},{10,11... | collective-permute-start | bytes 221192 | tf_op jit(solution)/shard_map/ppermute | solution.py:273
  216.9 5.2 %collective-permute-start.9 = (bf16[4,32,512]{2,1,0:T(8,128)(2,1)S(1)}, bf16[4,32,512]{2,1,0:T(8,128)(2,1)S(1)}, u32[]{:S(2)}, u32[]{:S(2)}) collective-permute-start(bf16[4,32,512]{2,1,0:T(8,128)(2,1)S(1)} %get-tuple-element.14), channel_id=1, source_target_pairs={{0,124},{1,125},{2,126},{3,127},{4,0},{5,1},{6,2},{7,3},{8,4},{9,5... | collective-permute-start | bytes 393224 | tf_op jit(solution)/shard_map/ppermute | solution.py:273
  217.0 10.7 %collective-permute-start.8 = (bf16[4,32,512]{2,1,0:T(8,128)(2,1)S(1)}, bf16[4,32,512]{2,1,0:T(8,128)(2,1)S(1)}, u32[]{:S(2)}, u32[]{:S(2)}) collective-permute-start(bf16[4,32,512]{2,1,0:T(8,128)(2,1)S(1)} %get-tuple-element.15), channel_id=1, source_target_pairs={{0,4},{1,5},{2,6},{3,7},{4,8},{5,9},{6,10},{7,11},{8,12},{9,13},{1... | collective-permute-start | bytes 393224 | tf_op jit(solution)/shard_map/ppermute | solution.py:273
  222.0 11.2 %copy-start.3 = (bf16[4,32,512]{2,1,0:T(8,128)(2,1)}, bf16[4,32,512]{2,1,0:T(8,128)(2,1)S(1)}, u32[]{:S(2)}) copy-start(bf16[4,32,512]{2,1,0:T(8,128)(2,1)S(1)} %collective-permute-done.9.east_ref) | copy-start | bytes 393220
  227.6 5.7 %copy-start.5 = (bf16[4,32,512]{2,1,0:T(8,128)(2,1)}, bf16[4,32,512]{2,1,0:T(8,128)(2,1)S(1)}, u32[]{:S(2)}) copy-start(bf16[4,32,512]{2,1,0:T(8,128)(2,1)S(1)} %collective-permute-done.8.west_ref) | copy-start | bytes 393220
  227.7 4.1 %collective-permute-start.11 = (bf16[4,18,512]{2,1,0:T(8,128)(2,1)S(1)}, bf16[4,18,512]{2,1,0:T(8,128)(2,1)S(1)}, u32[]{:S(2)}, u32[]{:S(2)}) collective-permute-start(bf16[4,18,512]{2,1,0:T(8,128)(2,1)S(1)} %get-tuple-element.43), channel_id=1, source_target_pairs={{0,64},{1,2},{2,1},{3,67},{4,68},{5,6},{6,5},{7,71},{8,72},{9,10},... | collective-permute-start | bytes 221192 | tf_op jit(solution)/shard_map/ppermute | solution.py:273
  228.7 3.8 %collective-permute-start.10 = (bf16[4,18,512]{2,1,0:T(8,128)(2,1)S(1)}, bf16[4,18,512]{2,1,0:T(8,128)(2,1)S(1)}, u32[]{:S(2)}, u32[]{:S(2)}) collective-permute-start(bf16[4,18,512]{2,1,0:T(8,128)(2,1)S(1)} %get-tuple-element.44), channel_id=1, source_target_pairs={{0,1},{1,0},{2,3},{3,2},{4,5},{5,4},{6,7},{7,6},{8,9},{9,8},{10,11... | collective-permute-start | bytes 221192 | tf_op jit(solution)/shard_map/ppermute | solution.py:273
